TPU v7x, 32 devices: a whole 2x2x4 slice. The times are simulated.
32 devices in a mesh: dp: 8 (over z, x), slab: 4 (over y, core).
Axes of the slice: x: 2, y: 2, z: 4, core: 2. Of those that a mesh axis runs over, the one named last changes fastest.
Arguments:
- inputs: bfloat16 [8, 24, 34944], P('dp', 'slab'), may hold values from -40 to 40
- upstream: bfloat16 [8, 24, 34944], P('dp', 'slab'), may hold values from -96 to 96
- labels: int32 [8, 24, 48], P('dp', 'slab'), may hold values from 0 to 2
- class_weights: float32 [3], replicated, may hold values from 0.25 to 4
- depth_kernel: bfloat16 [9, 728], replicated, may hold values from -2 to 2
- point_weight: bfloat16 [728, 728], replicated, may hold values from -0.21875 to 0.21875
- gain: float32 [728], replicated, may hold values from 0.5 to 1.5
- shift: float32 [728], replicated, may hold values from -3 to 3
Outputs:
- block_out: bfloat16 [8, 24, 34944], P('dp', 'slab')
- grad_input: bfloat16 [8, 24, 34944], P('dp', 'slab')
- grad_pointwise: float32 [728, 728], P(None, 'slab')
- grad_depthwise: float32 [9, 728], P(None, 'slab')
- grad_gain: float32 [728], P('slab')
- grad_shift: float32 [728], P('slab')
All inputs are finite; a program needn't handle non-finite values.
Results may differ from a plain program's by a relative error of at most 0.0052.
The roundings to bfloat16 on the way count: a program that leaves them out, or rounds other values in their place, can miss the bound.
Values may be sent and summed in bfloat16 or wider, within the bound.
No kernel may reach another device: no remote copies, remote signals or barrier semaphores. Data moves between devices by JAX's collectives and lax.ppermute only.
A program may use at most 64 MiB of HBM per device.

v0:
```python
import jax
import jax.numpy as jnp
from jax import lax
from jax.sharding import PartitionSpec as P


def padded_2(cells, sides, width):
    for axis, dim in sides:
        count = lax.axis_size(axis)
        ends = count - 1
        head = lax.slice_in_dim(cells, 0, width, axis=dim)
        tail = lax.slice_in_dim(cells, cells.shape[dim] - width, cells.shape[dim], axis=dim)
        cells = jnp.concatenate(
            [
                lax.ppermute(tail, axis, [(i, (i + 1) % count) for i in range(ends)]),
                cells,
                lax.ppermute(head, axis, [((i + 1) % count, i) for i in range(ends)]),
            ],
            axis=dim,
        )
    return cells


def widen_columns(values):
    return jnp.pad(values, ((0, 0), (0, 0), (1, 1), (0, 0)))


def depthwise(padded, kernel):
    row_count = padded.shape[1] - 2
    col_count = padded.shape[2]
    widened = widen_columns(padded)
    summed = jnp.zeros((padded.shape[0], row_count, col_count, padded.shape[3]), jnp.float32)
    for row_tap in range(3):
        for col_tap in range(3):
            window = widened[:, row_tap : row_tap + row_count, col_tap : col_tap + col_count, :]
            summed = summed + window.astype(jnp.float32) * kernel[3 * row_tap + col_tap].astype(
                jnp.float32
            )
    return summed


def transposed(padded_grad, kernel):
    row_count = padded_grad.shape[1] - 2
    col_count = padded_grad.shape[2]
    widened = widen_columns(padded_grad)
    summed = jnp.zeros(
        (padded_grad.shape[0], row_count, col_count, padded_grad.shape[3]), jnp.float32
    )
    for row_tap in range(3):
        for col_tap in range(3):
            window = widened[
                :, 2 - row_tap : 2 - row_tap + row_count, 2 - col_tap : 2 - col_tap + col_count, :
            ]
            summed = summed + window.astype(jnp.float32) * kernel[3 * row_tap + col_tap].astype(
                jnp.float32
            )
    return summed


def taps(padded, grad_image):
    row_count = grad_image.shape[1]
    col_count = grad_image.shape[2]
    widened = widen_columns(padded)
    results = []
    for row_tap in range(3):
        for col_tap in range(3):
            window = widened[:, row_tap : row_tap + row_count, col_tap : col_tap + col_count, :]
            results.append(
                jnp.einsum("srwc,srwc->c", window, grad_image, preferred_element_type=jnp.float32)
            )
    return jnp.stack(results)


def rows_around(values):
    return padded_2(values, (("slab", 1),), 1)


def slab_totals(first, second):
    return lax.psum((first, second), "slab")


def local(inputs, upstream, labels, class_weights, depth_kernel, point_weight, gain, shift):
    samples, row_count, flat_width = inputs.shape
    channels = point_weight.shape[0]
    col_count = flat_width // channels
    pieces = lax.axis_size("slab")
    share = channels // pieces
    sample = inputs.reshape(samples, row_count, col_count, channels)
    active = jnp.maximum(sample, 0)
    padded = rows_around(active)
    depth = depthwise(padded, depth_kernel).astype(jnp.bfloat16)
    flat_depth = depth.reshape(-1, channels)
    projected = jnp.dot(flat_depth, point_weight, preferred_element_type=jnp.float32)
    match = labels.reshape(-1)[:, None] == jnp.arange(3, dtype=jnp.int32)[None, :]
    weight = jnp.sum(jnp.where(match, class_weights[None, :], 0.0), axis=1)
    grad_out = upstream.reshape(-1, channels).astype(jnp.float32) * weight[:, None]
    count = projected.shape[0] * pieces
    proj_sum, shift_part = slab_totals(jnp.sum(projected, axis=0), jnp.sum(grad_out, axis=0))
    center = proj_sum / count
    deviation = projected - center
    square_sum, cross = slab_totals(
        jnp.sum(deviation * deviation, axis=0), jnp.sum(grad_out * deviation, axis=0)
    )
    spread = square_sum / count
    inverse = lax.rsqrt(spread + 1e-05)
    normed = (projected - center) * inverse
    gain_part = cross * inverse
    result = sample.reshape(-1, channels).astype(jnp.float32) + gain * normed + shift
    grad_proj = (
        gain * inverse * (grad_out - shift_part / count - normed * gain_part / count)
    ).astype(jnp.bfloat16)
    grad_depth = lax.dot_general(
        grad_proj, point_weight, (((1,), (1,)), ((), ())), preferred_element_type=jnp.float32
    ).astype(jnp.bfloat16)
    grad_image = grad_depth.reshape(depth.shape)
    padded_grad = rows_around(grad_image)
    grad_active = transposed(padded_grad, depth_kernel).reshape(-1, channels)
    grad_input = grad_out + jnp.where(sample.reshape(-1, channels) > 0, grad_active, 0.0)
    tap_local = taps(padded, grad_image)
    columns = lax.all_to_all(grad_proj, "slab", split_axis=1, concat_axis=0, tiled=True)
    point_share = lax.dot_general(
        lax.all_gather(flat_depth, "slab", axis=0, tiled=True),
        columns,
        (((0,), (0,)), ((), ())),
        preferred_element_type=jnp.float32,
    )
    tap_share = lax.psum_scatter(tap_local, "slab", scatter_dimension=1, tiled=True)
    offset = lax.axis_index("slab") * share
    gain_share = lax.dynamic_slice_in_dim(gain_part, offset, share, 0)
    shift_share = lax.dynamic_slice_in_dim(shift_part, offset, share, 0)
    point_sum, tap_sum, gain_sum, shift_sum = lax.psum(
        (point_share, tap_share, gain_share, shift_share), "dp"
    )
    batch = samples * lax.axis_size("dp")
    block_out = result.astype(jnp.bfloat16).reshape(samples, row_count, flat_width)
    grad_in = grad_input.astype(jnp.bfloat16).reshape(samples, row_count, flat_width)
    return (
        block_out,
        grad_in,
        point_sum / batch,
        tap_sum / batch,
        gain_sum / batch,
        shift_sum / batch,
    )


def solution(mesh):
    return jax.shard_map(
        local,
        mesh=mesh,
        in_specs=(
            P("dp", "slab", None),
            P("dp", "slab", None),
            P("dp", "slab", None),
            P(),
            P(),
            P(),
            P(),
            P(),
        ),
        out_specs=(
            P("dp", "slab", None),
            P("dp", "slab", None),
            P(None, "slab"),
            P(None, "slab"),
            P("slab"),
            P("slab"),
        ),
        check_vma=False,
    )
```

profile of v0, /device:TPU:0, one launch (start us, length us, event | category | flops | bytes accessed | tf_op | source)
XLA Modules:
  0.0 208.4 jit_solution(1864434515289965982)
XLA Ops:
  7.2 1.2 broadcast_maximum_fusion
  8.5 1.1 max.27
  10.3 2.3 %collective-permute-start = (bf16[1,1,48,728]{3,2,1,0:T(8,128)(2,1)}, bf16[1,1,48,728]{3,2,1,0:T(8,128)(2,1)S(1)}, u32[]{:S(2)}, u32[]{:S(2)}) collective-permute-start(bf16[1,1,48,728]{3,2,1,0:T(8,128)(2,1)} %get-tuple-element.39), channel_id=1, source_target_pairs={{0,1},{1,2},{2,3},{4,5},{5,6},{6,7},{8,9},{9,10},{10,11},{12,13},{... | collective-permute-start | bytes 209672 | tf_op jit(solution)/shard_map/ppermute | solution.py:15
  12.6 1.3 collective-permute-start.1
  14.0 2.0 reshape.241
  16.0 1.9 max.28
  18.0 1.1 reshape.251
  20.0 1.8 mul.233
  23.0 1.1 convert_reduce_fusion.8
  24.4 1.4 add_convert_fusion.2
  25.9 2.4 %fusion.17 = (f32[728]{0:T(1024)S(1)}, f32[288,728]{1,0:T(8,128)}) fusion(bf16[288,728]{1,0:T(8,128)(2,1)} %bitcast.78, bf16[728,728]{1,0:T(8,128)(2,1)S(1)} %copy-done), kind=kOutput, calls=%fused_computation.65 | convolution fusion | flops 305479712 | bytes 2320864 | tf_op jit(solution)/shard_map/dot_general | solution.py:93
  28.4 9.0 %psum.56 = f32[728]{0:T(1024)S(1)} all-reduce(f32[728]{0:T(1024)S(1)} %get-tuple-element.44), channel_id=1, replica_groups=mesh['dp'=8,'slab'=4] {'slab'}, use_global_device_ids=true, to_apply=%region_1.2 | all-reduce | flops 728 | bytes 5824 | tf_op jit(solution)/shard_map/psum | solution.py:79
  37.4 1.4 multiply_reduce_fusion
  38.9 12.1 %all-reduce.4 = (f32[728]{0:T(1024)S(1)}, f32[728]{0:T(1024)S(1)}, f32[728]{0:T(1024)S(1)}) all-reduce(f32[728]{0:T(1024)S(1)} %get-tuple-element.13, f32[728]{0:T(1024)S(1)} %get-tuple-element.12, f32[728]{0:T(1024)S(1)} %get-tuple-element.14), channel_id=1, replica_groups=mesh['dp'=8,'slab'=4] {'slab'}, use_global_device_ids=true, to_apply=%region_3.4 | all-reduce | flops 2184 | bytes 17472 | tf_op jit(solution)/shard_map/psum | solution.py:79
  51.1 2.6 %multiply_convert_fusion = (bf16[288,728]{1,0:T(8,128)(2,1)S(1)}, bf16[288,728]{1,0:T(8,128)(2,1)}) fusion(f32[288,728]{1,0:T(8,128)S(1)} %reshape.251, f32[288,728]{1,0:T(8,128)} %get-tuple-element.45, f32[728]{0:T(1024)S(1)} %get-tuple-element.42, f32[728]{0:T(1024)S(1)} %get-tuple-element.46, f32[288]{0:T(512)S(1)} %copy-done.25, ...), kind=kLoop, calls=%fused_computation.24 | loop fusion | flops 2725632 | bytes 3376160 | tf_op jit(solution)/shard_map/convert_element_type | solution.py:111
  55.0 0.8 fusion.9
  56.0 1.3 collective-permute-start.2
  57.3 1.3 collective-permute-start.3
  58.7 12.6 %all-reduce.2 = f32[9,728]{1,0:T(8,128)S(1)} all-reduce(f32[9,728]{1,0:T(8,128)S(1)} %stack.39), channel_id=2, replica_groups=mesh['dp'=8,'slab'=4] {'slab'}, use_global_device_ids=true, to_apply=%region_10.11.clone | all-reduce | flops 6552 | bytes 52416
  71.3 37.4 %all-reduce.3 = (f32[9,182]{1,0:T(8,128)S(1)}, f32[182]{0:T(256)S(1)}, f32[182]{0:T(256)S(1)}) all-reduce(f32[9,182]{1,0:T(8,128)S(1)} %constant_dynamic-slice_fusion, f32[182]{0:T(256)S(1)} %dynamic_slice.6, f32[182]{0:T(256)S(1)} %dynamic_slice.7), channel_id=1, replica_groups=mesh['dp'=8,'slab'=4] {'dp'}, use_global_device_ids=true, to_apply=%region_11.12 | all-reduce | flops 2002 | bytes 16016 | tf_op jit(solution)/shard_map/psum | solution.py:131
  110.5 1.5 all_to_all.14
  112.0 1.6 copy.17
  113.5 3.5 %all-to-all-start = ((bf16[288,4,182]{0,2,1:T(8,128)(2,1)}), bf16[288,4,182]{0,2,1:T(8,128)(2,1)S(1)}, u32[]{:S(2)}, u32[]{:S(2)}) async-start(bf16[288,4,182]{0,2,1:T(8,128)(2,1)} %copy.17), calls=%async_computation | async-start | bytes 1130496 | tf_op jit(solution)/shard_map/all_to_all | solution.py:120
  117.3 1.7 reshape.229
  119.9 1.6 multiply_add_fusion
  121.5 1.7 reshape.231
  123.2 3.1 %all-to-all-done = bf16[288,4,182]{0,2,1:T(8,128)(2,1)S(1)} async-done(((bf16[288,4,182]{0,2,1:T(8,128)(2,1)}), bf16[288,4,182]{0,2,1:T(8,128)(2,1)S(1)}, u32[]{:S(2)}, u32[]{:S(2)}) %all-to-all-start) | async-done | bytes 419360 | tf_op jit(solution)/shard_map/all_to_all | solution.py:120
  126.5 1.3 all_to_all.17
  127.8 3.0 %fusion.18 = f32[728,182]{0,1:T(8,128)} fusion(bf16[1152,728]{1,0:T(8,128)(2,1)} %all-gather.2.cloned.1.call-done, bf16[1152,182]{0,1:T(8,128)(2,1)} %all_to_all.17), kind=kOutput, calls=%fused_computation.66 | convolution fusion | flops 305270784 | bytes 2626624 | tf_op jit(solution)/shard_map/dot_general | solution.py:121
  130.8 2.4 %add_convert_fusion = bf16[1,6,34944]{2,1,0:T(8,128)(2,1)} fusion(f32[1,6,34944]{2,1,0:T(8,128)} %reshape.231, f32[1,6,34944]{2,1,0:T(8,128)S(1)} %copy-done.3, bf16[1,6,34944]{2,1,0:T(8,128)(2,1)S(1)} %copy-done.2, bf16[1,6,34944]{2,1,0:T(8,128)(2,1)S(1)} %copy-done.5), kind=kLoop, calls=%fused_computation.13 | loop fusion | flops 1257984 | bytes 2935296 | tf_op jit(solution)/shard_map/convert_element_type | solution.py:136
  133.2 66.4 %all-reduce.7.cloned.1.call-done = f32[728,182]{0,1:T(8,128)} async-done(((f32[728,182]{0,1:T(8,128)}), f32[728,182]{0,1:T(8,128)}) %all-reduce.7.cloned.1.call-update) | async-done | bytes 530000 | tf_op jit(solution)/shard_map/psum | solution.py:131
  199.6 1.9 broadcast_multiply_fusion
  (101 shorter events, 7.3 us)
Async XLA Ops:
  7.2 18.7 %copy-start = (bf16[728,728]{1,0:T(8,128)(2,1)S(1)}, bf16[728,728]{1,0:T(8,128)(2,1)}, u32[]{:S(2)}) copy-start(bf16[728,728]{1,0:T(8,128)(2,1)} %param.13) | copy-start | bytes 3179908
  7.2 6.8 %copy-start.1 = (bf16[1,6,34944]{2,1,0:T(8,128)(2,1)S(1)}, bf16[1,6,34944]{2,1,0:T(8,128)(2,1)}, u32[]{:S(2)}) copy-start(bf16[1,6,34944]{2,1,0:T(8,128)(2,1)} %param.8) | copy-start | bytes 1257988
  7.2 120.6 %all-gather.2.cloned.1.call-start = ((), (), s32[]{:S(2)}) async-start(), calls=%async_computation.1 | async-start | bytes 2211840 | tf_op jit(solution)/shard_map/all_gather | solution.py:122
  9.6 8.3 %copy-start.28 = (s32[1,6,48]{2,0,1:T(1,128)S(1)}, s32[1,6,48]{2,0,1:T(1,128)}, u32[]{:S(2)}) copy-start(s32[1,6,48]{2,0,1:T(1,128)} %param.10) | copy-start | bytes 3460
  9.6 8.4 %copy-start.4 = (bf16[1,6,34944]{2,1,0:T(8,128)(2,1)S(1)}, bf16[1,6,34944]{2,1,0:T(8,128)(2,1)}, u32[]{:S(2)}) copy-start(bf16[1,6,34944]{2,1,0:T(8,128)(2,1)} %param.9) | copy-start | bytes 1257988
  10.3 13.9 %collective-permute-start = (bf16[1,1,48,728]{3,2,1,0:T(8,128)(2,1)}, bf16[1,1,48,728]{3,2,1,0:T(8,128)(2,1)S(1)}, u32[]{:S(2)}, u32[]{:S(2)}) collective-permute-start(bf16[1,1,48,728]{3,2,1,0:T(8,128)(2,1)} %get-tuple-element.39), channel_id=1, source_target_pairs={{0,1},{1,2},{2,3},{4,5},{5,6},{6,7},{8,9},{9,10},{10,11},{12,13},{... | collective-permute-start | bytes 209672 | tf_op jit(solution)/shard_map/ppermute | solution.py:15
  12.6 11.5 %collective-permute-start.1 = (bf16[1,1,48,728]{3,2,1,0:T(8,128)(2,1)S(1)}, bf16[1,1,48,728]{3,2,1,0:T(8,128)(2,1)S(1)}, u32[]{:S(2)}, u32[]{:S(2)}) collective-permute-start(bf16[1,1,48,728]{3,2,1,0:T(8,128)(2,1)S(1)} %get-tuple-element.40), channel_id=1, source_target_pairs={{1,0},{2,1},{3,2},{5,4},{6,5},{7,6},{9,8},{10,9},{11,10},{13,12},{... | collective-permute-start | bytes 209672 | tf_op jit(solution)/shard_map/ppermute | solution.py:17
  16.0 3.1 %copy-start.29 = (f32[3]{0:T(128)S(1)}, f32[3]{0:T(128)}, u32[]{:S(2)}) copy-start(f32[3]{0:T(128)} %param.11) | copy-start | bytes 40
  20.0 1.8 copy-start.30
  24.1 1.8 copy-start.10
  24.1 1.7 copy-start.12
  24.1 1.7 copy-start.14
  24.1 1.7 copy-start.16
  24.1 1.7 copy-start.18
  24.1 1.7 copy-start.20
  25.9 11.5 %copy-start.25 = (f32[288]{0:T(512)S(1)}, f32[288]{0:T(512)}, u32[]{:S(2)}) copy-start(f32[288]{0:T(512)} %copy-done.24) | copy-start | bytes 3460
  28.4 22.6 %copy-start.26 = (f32[728]{0:T(1024)S(1)}, f32[728]{0:T(1024)}, u32[]{:S(2)}) copy-start(f32[728]{0:T(1024)} %param.14) | copy-start | bytes 8740
  28.4 22.7 %copy-start.27 = (f32[728]{0:T(1024)S(1)}, f32[728]{0:T(1024)}, u32[]{:S(2)}) copy-start(f32[728]{0:T(1024)} %param.15) | copy-start | bytes 8740
  56.0 63.0 %collective-permute-start.2 = (bf16[1,1,48,728]{3,2,1,0:T(8,128)(2,1)S(1)}, bf16[1,1,48,728]{3,2,1,0:T(8,128)(2,1)S(1)}, u32[]{:S(2)}, u32[]{:S(2)}) collective-permute-start(bf16[1,1,48,728]{3,2,1,0:T(8,128)(2,1)S(1)} %get-tuple-element.37), channel_id=1, source_target_pairs={{0,1},{1,2},{2,3},{4,5},{5,6},{6,7},{8,9},{9,10},{10,11},{12,13},{... | collective-permute-start | bytes 209672 | tf_op jit(solution)/shard_map/ppermute | solution.py:15
  57.3 61.8 %collective-permute-start.3 = (bf16[1,1,48,728]{3,2,1,0:T(8,128)(2,1)S(1)}, bf16[1,1,48,728]{3,2,1,0:T(8,128)(2,1)S(1)}, u32[]{:S(2)}, u32[]{:S(2)}) collective-permute-start(bf16[1,1,48,728]{3,2,1,0:T(8,128)(2,1)S(1)} %get-tuple-element.38), channel_id=1, source_target_pairs={{1,0},{2,1},{3,2},{5,4},{6,5},{7,6},{9,8},{10,9},{11,10},{13,12},{... | collective-permute-start | bytes 209672 | tf_op jit(solution)/shard_map/ppermute | solution.py:17
  112.0 5.4 %copy-start.7 = (bf16[288,728]{1,0:T(8,128)(2,1)S(1)}, bf16[288,728]{1,0:T(8,128)(2,1)}, u32[]{:S(2)}) copy-start(bf16[288,728]{1,0:T(8,128)(2,1)} %get-tuple-element.36) | copy-start | bytes 1257988
  113.5 12.7 %all-to-all-start = ((bf16[288,4,182]{0,2,1:T(8,128)(2,1)}), bf16[288,4,182]{0,2,1:T(8,128)(2,1)S(1)}, u32[]{:S(2)}, u32[]{:S(2)}) async-start(bf16[288,4,182]{0,2,1:T(8,128)(2,1)} %copy.17), calls=%async_computation | async-start | bytes 1130496 | tf_op jit(solution)/shard_map/all_to_all | solution.py:120
  117.0 2.8 %copy-start.11 = (f32[728]{0:T(1024)S(1)}, f32[728]{0:T(1024)}, u32[]{:S(2)}) copy-start(f32[728]{0:T(1024)} %copy-done.10) | copy-start | bytes 8740
  117.0 2.8 %copy-start.13 = (f32[728]{0:T(1024)S(1)}, f32[728]{0:T(1024)}, u32[]{:S(2)}) copy-start(f32[728]{0:T(1024)} %copy-done.12) | copy-start | bytes 8740
  117.0 2.8 %copy-start.15 = (f32[728]{0:T(1024)S(1)}, f32[728]{0:T(1024)}, u32[]{:S(2)}) copy-start(f32[728]{0:T(1024)} %copy-done.14) | copy-start | bytes 8740
  117.1 2.8 %copy-start.17 = (f32[728]{0:T(1024)S(1)}, f32[728]{0:T(1024)}, u32[]{:S(2)}) copy-start(f32[728]{0:T(1024)} %copy-done.16) | copy-start | bytes 8740
  117.1 2.8 %copy-start.19 = (f32[728]{0:T(1024)S(1)}, f32[728]{0:T(1024)}, u32[]{:S(2)}) copy-start(f32[728]{0:T(1024)} %copy-done.18) | copy-start | bytes 8740
  117.1 2.8 %copy-start.21 = (f32[728]{0:T(1024)S(1)}, f32[728]{0:T(1024)}, u32[]{:S(2)}) copy-start(f32[728]{0:T(1024)} %copy-done.20) | copy-start | bytes 8740
  117.1 82.5 %all-reduce.7.cloned.1.call-start = ((), (), s32[]{:S(2)}) async-start(), calls=%async_computation.2 | async-start | bytes 1130496 | tf_op jit(solution)/shard_map/psum | solution.py:131
  127.7 3.1 %copy-start.2 = (bf16[1,6,34944]{2,1,0:T(8,128)(2,1)S(1)}, bf16[1,6,34944]{2,1,0:T(8,128)(2,1)}, u32[]{:S(2)}) copy-start(bf16[1,6,34944]{2,1,0:T(8,128)(2,1)} %param.8) | copy-start | bytes 1257988
  127.7 3.1 %copy-start.3 = (f32[1,6,34944]{2,1,0:T(8,128)S(1)}, f32[1,6,34944]{2,1,0:T(8,128)}, u32[]{:S(2)}) copy-start(f32[1,6,34944]{2,1,0:T(8,128)} %mul.233) | copy-start | bytes 2515972
  127.8 3.1 %copy-start.5 = (bf16[1,6,34944]{2,1,0:T(8,128)(2,1)S(1)}, bf16[1,6,34944]{2,1,0:T(8,128)(2,1)}, u32[]{:S(2)}) copy-start(bf16[1,6,34944]{2,1,0:T(8,128)(2,1)} %param.9) | copy-start | bytes 1257988
  (6 other events, 6.7 us)
Sparse Core Ops, SparseCore 0:
  26.0 25.5 all-gather.1
  130.9 68.6 all-reduce.6
where the time goes:
time: 209 us; the launch traced here: 208 us
  blocking collectives  71.1 us (34%)
  waiting for transfers between devices  69.5 us (33%)
  local copies, waits for them, and re-layouts  19.8 us (9%)
  other arithmetic  16.7 us (8%)
  between operations  15.3 us (7%)
  starting transfers between devices  9.96 us (5%)
  matrix products  6.02 us (3%)
    psum x1, waiting for transfers between devices, local(): lax.psum((point_share, tap_share, gain_share, shift_share), 'dp')  66.4 us
    psum x1, blocking collectives, local(): lax.psum((point_share, tap_share, gain_share, shift_share), 'dp')  37.4 us
    psum x2, blocking collectives, slab_totals(): return lax.psum((first, second), 'slab')  21.1 us
    unnamed x1, blocking collectives  12.6 us
    all_to_all x4, local copies, waits for them, and re-layouts, local(): lax.all_to_all(grad_proj, 'slab', split_axis=1, concat_axis=0, tiled=True)  4.52 us
  transfers between devices with their start and end apart: 7, of which 2 were waited for; matrix products, arithmetic and copies ran while one was open for 14% of the time, Pallas kernels for 0%

commit v1 on v0

v1 whole, which is shorter than its diff:
```python
import functools

import jax
import jax.numpy as jnp
from jax import lax
from jax.experimental import pallas as pl
from jax.experimental.pallas import tpu as pltpu
from jax.sharding import PartitionSpec as P

F32 = jnp.float32
BF16 = jnp.bfloat16
LANES = 128
SUB = 8
EPS = 1e-05


def round_up(value, unit):
    return -(-value // unit) * unit


def tiles(width):
    return [(start, min(LANES, width - start)) for start in range(0, width, LANES)]


def share_order(pieces):
    return [2 * j + parity for parity in range(2) for j in range(pieces // 2)]


def to_shares(values, pieces, padded):
    share = values.shape[1] // pieces
    gap = padded // pieces - share
    parts = []
    for owner in share_order(pieces):
        parts.append(values[:, owner * share : (owner + 1) * share])
        if gap:
            parts.append(jnp.zeros((values.shape[0], gap), values.dtype))
    return jnp.concatenate(parts, axis=1)


def from_shares(values, pieces, channels):
    share = channels // pieces
    slot = values.shape[1] // pieces
    order = share_order(pieces)
    parts = []
    for owner in range(pieces):
        start = order.index(owner) * slot
        parts.append(values[:, start : start + share])
    return jnp.concatenate(parts, axis=1)


def column(ref, col, channels):
    start = col * channels
    base = start // LANES * LANES
    off = start - base
    end = min(ref.shape[1], base + round_up(off + channels, LANES))
    return ref[:, base:end].astype(F32)[:, off : off + channels]


def prepare_kernel(pieces, weights, x_ref, u_ref, label_ref, kernel_ref, point_ref, image_ref, part_ref, grad_ref, group_ref, spread_ref):
    rows, cols = label_ref.shape
    channels = point_ref.shape[0]
    sub = image_ref.shape[1]
    padded = spread_ref.shape[1]
    share, slot = channels // pieces, padded // pieces
    out_col = lax.broadcasted_iota(jnp.int32, (channels, padded), 1)
    in_row = lax.broadcasted_iota(jnp.int32, (channels, padded), 0)
    place = out_col // slot
    inside = out_col - place * slot
    owner = jnp.where(place >= pieces // 2, 2 * place - pieces + 1, 2 * place)
    chosen = (in_row == owner * share + inside) & (inside < share)
    picks = jnp.where(chosen, 1.0, 0.0).astype(BF16)
    spread_ref[...] = jnp.dot(point_ref[...], picks, preferred_element_type=F32).astype(BF16)
    labels = label_ref[...]
    weight = jnp.where(labels == 0, weights[0], jnp.where(labels == 1, weights[1], jnp.where(labels == 2, weights[2], 0.0)))
    for col in range(cols):
        values = column(x_ref, col, channels)
        image_ref[col, :rows, :] = values
        image_ref[col, rows:, :] = jnp.zeros((sub - rows, channels), F32)
        grads = column(u_ref, col, channels) * weight[:, col : col + 1]
        grad_ref[col, :rows, :] = grads
        grad_ref[col, rows:, :] = jnp.zeros((sub - rows, channels), F32)
        group_ref[col * sub : col * sub + rows, :] = to_shares(grads, pieces, padded)
        group_ref[col * sub + rows : (col + 1) * sub, :] = jnp.zeros((sub - rows, padded), F32)
    for start, width in tiles(channels):
        at = pl.ds(start, width)
        taps = [kernel_ref[t : t + 1, at].astype(F32) for t in range(9)]
        before = jnp.zeros((sub, width), F32)
        pending = before
        for col in range(cols):
            mid = jnp.maximum(image_ref[col, :, at], 0.0)
            up = pltpu.roll(mid, 1, 0)
            down = pltpu.roll(mid, sub - 1, 0)
            sums = [taps[j] * up + taps[3 + j] * mid + taps[6 + j] * down for j in range(3)]
            if col:
                part_ref[col - 1, :, at] = pending + sums[2]
            pending = before + sums[1]
            before = sums[0]
        part_ref[cols - 1, :, at] = pending


def forward_kernel(pieces, where_ref, part_ref, image_ref, one_ref, two_ref, kernel_ref, spread_ref, group_ref, depth_ref, proj_ref, active_ref, stats_ref, sums_ref, rows):
    cols, sub, channels = part_ref.shape
    padded = spread_ref.shape[1]
    even = where_ref[0] % 2 == 0
    has_top = jnp.where(where_ref[0] > 0, 1.0, 0.0)
    has_bottom = jnp.where(where_ref[0] < pieces - 1, 1.0, 0.0)
    line = lax.broadcasted_iota(jnp.int32, (sub, channels), 0)
    wide = [
        jnp.where(line == 0, kernel_ref[j : j + 1, :].astype(F32), kernel_ref[6 + j : 7 + j, :].astype(F32))
        for j in range(3)
    ]
    for col in range(cols):
        one = jnp.maximum(column(one_ref, col, channels), 0.0)
        two = jnp.maximum(column(two_ref, col, channels), 0.0)
        top = jnp.where(even, two, one) * has_top
        bottom = jnp.where(even, one, two) * has_bottom
        own = jnp.maximum(image_ref[col], 0.0)
        active_ref[col] = jnp.where(line == rows, bottom, jnp.where(line == sub - 1, top, own))
        sums_ref[col] = jnp.where(line == 0, top, jnp.where(line == rows - 1, bottom, 0.0))
    for start, width in tiles(channels):
        at = pl.ds(start, width)
        inside = lax.broadcasted_iota(jnp.int32, (sub, width), 0) < rows
        taps = [w[:, start : start + width] for w in wide]
        before = jnp.zeros((sub, width), F32)
        pending = before
        for col in range(cols):
            halo = sums_ref[col, :, at]
            if col:
                sums_ref[col - 1, :, at] = jnp.where(inside, part_ref[col - 1, :, at] + pending + taps[2] * halo, 0.0)
            pending = before + taps[1] * halo
            before = taps[0] * halo
        sums_ref[cols - 1, :, at] = jnp.where(inside, part_ref[cols - 1, :, at] + pending, 0.0)
    depth = sums_ref[...].reshape(cols * sub, channels).astype(BF16)
    depth_ref[...] = depth
    proj_ref[...] = jnp.dot(depth, spread_ref[...], preferred_element_type=F32)
    count = rows * cols
    for start, width in tiles(padded):
        at = pl.ds(start, width)
        proj = proj_ref[:, at]
        grads = group_ref[:, at]
        mine = lax.broadcasted_iota(jnp.int32, (cols * sub, width), 0) % sub < rows
        center = jnp.sum(proj, axis=0, keepdims=True) / count
        deviation = jnp.where(mine, proj - center, 0.0)
        stats_ref[0:1, at] = center
        stats_ref[1:2, at] = jnp.sum(deviation * deviation, axis=0, keepdims=True)
        stats_ref[2:3, at] = jnp.sum(grads, axis=0, keepdims=True)
        stats_ref[3:4, at] = jnp.sum(grads * deviation, axis=0, keepdims=True)
        stats_ref[4:SUB, at] = jnp.zeros((SUB - 4, width), F32)


def cotangent_kernel(pieces, rows, cols, where_ref, stats_ref, proj_ref, group_ref, gain_ref, shift_ref, full_ref, keep_ref, send_ref, norm_ref):
    padded = proj_ref.shape[1]
    sub = proj_ref.shape[0] // cols
    local = rows * cols
    count = local * pieces
    stats = [stats_ref[p * SUB : p * SUB + 4, :] for p in range(pieces)]
    center = sum(s[0:1] for s in stats) / pieces
    square = sum(s[1:2] + local * (s[0:1] - center) ** 2 for s in stats)
    shift_part = sum(s[2:3] for s in stats)
    cross = sum(s[3:4] + (s[0:1] - center) * s[2:3] for s in stats)
    inverse = lax.rsqrt(square / count + EPS)
    gain_part = cross * inverse
    gain = to_shares(gain_ref[...], pieces, padded)
    norm_ref[0:1, :] = center
    norm_ref[1:2, :] = inverse
    norm_ref[2:3, :] = gain
    norm_ref[3:4, :] = to_shares(shift_ref[...], pieces, padded)
    norm_ref[4:5, :] = gain_part
    norm_ref[5:6, :] = shift_part
    norm_ref[6:8, :] = jnp.zeros((2, padded), F32)
    for start, width in tiles(padded):
        at = slice(start, start + width)
        mine = lax.broadcasted_iota(jnp.int32, (cols * sub, width), 0) % sub < rows
        normed = (proj_ref[:, start : start + width] - center[:, at]) * inverse[:, at]
        value = (gain * inverse)[:, at] * (
            group_ref[:, start : start + width] - (shift_part / count)[:, at] - normed * (gain_part / count)[:, at]
        )
        full_ref[:, start : start + width] = jnp.where(mine, value, 0.0).astype(BF16)
    even = where_ref[0] % 2 == 0
    half = padded // 2
    first, second = full_ref[:, :half], full_ref[:, half:]
    keep_ref[...] = jnp.where(even, first, second)
    send_ref[...] = jnp.where(even, second, first)


def backward_kernel(rows, full_ref, spread_ref, active_ref, where_ref, depth_grad_ref, tap_ref, one_ref, two_ref):
    cols, sub, channels = active_ref.shape
    grad = lax.dot_general(full_ref[...], spread_ref[...], (((1,), (1,)), ((), ())), preferred_element_type=F32)
    depth_grad_ref[...] = grad.astype(BF16).astype(F32).reshape(cols, sub, channels)
    even = where_ref[0] % 2 == 0
    first = depth_grad_ref[:, 0, :].astype(BF16)
    last = depth_grad_ref[:, rows - 1, :].astype(BF16)
    one_ref[...] = jnp.where(even, last, first)
    two_ref[...] = jnp.where(even, first, last)
    for start, width in tiles(channels):
        at = pl.ds(start, width)
        totals = [jnp.zeros((sub, width), F32) for _ in range(9)]
        zero = jnp.zeros((sub, width), F32)
        ahead = depth_grad_ref[0, :, at]
        here = zero
        for col in range(cols):
            behind, here = here, ahead
            ahead = depth_grad_ref[col + 1, :, at] if col + 1 < cols else zero
            mid = active_ref[col, :, at]
            shifted = (pltpu.roll(mid, 1, 0), mid, pltpu.roll(mid, sub - 1, 0))
            for i in range(3):
                for j, other in enumerate((ahead, here, behind)):
                    totals[3 * i + j] = totals[3 * i + j] + shifted[i] * other
        for t in range(9):
            tap_ref[t : t + 1, at] = jnp.sum(totals[t], axis=0, keepdims=True)
        tap_ref[9:, at] = jnp.zeros((tap_ref.shape[0] - 9, width), F32)


def product_kernel(mine_ref, theirs_ref, depth_ref, other_ref, out_ref):
    dims = (((0,), (0,)), ((), ()))
    out_ref[...] = lax.dot_general(mine_ref[...], depth_ref[...], dims, preferred_element_type=F32) + lax.dot_general(
        theirs_ref[...], other_ref[...], dims, preferred_element_type=F32
    )


def output_kernel(pieces, rows, where_ref, image_ref, grad_ref, proj_ref, norm_ref, depth_grad_ref, one_ref, two_ref, kernel_ref, block_ref, input_ref, halo_ref, flat_ref, flat2_ref):
    cols, sub, channels = image_ref.shape
    even = where_ref[0] % 2 == 0
    has_top = jnp.where(where_ref[0] > 0, 1.0, 0.0)
    has_bottom = jnp.where(where_ref[0] < pieces - 1, 1.0, 0.0)
    line = lax.broadcasted_iota(jnp.int32, (sub, channels), 0)
    one = one_ref[...].astype(F32)
    two = two_ref[...].astype(F32)
    top = jnp.where(even, two, one) * has_top
    bottom = jnp.where(even, one, two) * has_bottom
    center, inverse, gain, shift = (norm_ref[t : t + 1, :] for t in range(4))
    for col in range(cols):
        own = depth_grad_ref[col]
        halo_ref[col] = jnp.where(
            line == rows, bottom[col : col + 1], jnp.where(line == sub - 1, top[col : col + 1], own)
        )
    for start, width in tiles(channels):
        at = pl.ds(start, width)
        taps = [kernel_ref[t : t + 1, at].astype(F32) for t in range(9)]
        before = jnp.zeros((sub, width), F32)
        pending = before
        for col in range(cols):
            mid = halo_ref[col, :, at]
            up = pltpu.roll(mid, 1, 0)
            down = pltpu.roll(mid, sub - 1, 0)
            sums = [taps[j] * down + taps[3 + j] * mid + taps[6 + j] * up for j in range(3)]
            if col:
                last = pending + sums[0]
                image = image_ref[col - 1, :, at]
                halo_ref[col - 1, :, at] = grad_ref[col - 1, :, at] + jnp.where(image > 0, last, 0.0)
            pending = before + sums[1]
            before = sums[2]
        image = image_ref[cols - 1, :, at]
        halo_ref[cols - 1, :, at] = grad_ref[cols - 1, :, at] + jnp.where(image > 0, pending, 0.0)
    for col in range(cols):
        normed = (proj_ref[col * sub : (col + 1) * sub, :] - center) * inverse
        result = image_ref[col] + from_shares(gain * normed + shift, pieces, channels)
        flat_ref[:, col * channels : (col + 1) * channels] = result
        flat2_ref[:, col * channels : (col + 1) * channels] = halo_ref[col]
    block_ref[...] = flat_ref[:rows, :].astype(BF16)
    input_ref[...] = flat2_ref[:rows, :].astype(BF16)


def high_low(values):
    high = values.astype(BF16)
    return high, (values - high.astype(F32)).astype(BF16)


def call(body, outs, *args, smem=(), scratch=()):
    vmem = pl.BlockSpec(memory_space=pltpu.VMEM)
    specs = [pl.BlockSpec(memory_space=pltpu.SMEM) if i in smem else vmem for i in range(len(args))]
    return pl.pallas_call(
        body,
        out_shape=[jax.ShapeDtypeStruct(shape, dtype) for shape, dtype in outs],
        in_specs=specs,
        out_specs=[vmem] * len(outs),
        scratch_shapes=list(scratch),
        compiler_params=pltpu.CompilerParams(vmem_limit_bytes=32 * 1024 * 1024),
    )(*args)


def local(inputs, upstream, labels, class_weights, depth_kernel, point_weight, gain, shift):
    samples, rows, flat = inputs.shape
    assert samples == 1
    channels = point_weight.shape[0]
    cols = flat // channels
    pieces = lax.axis_size("slab")
    copies = lax.axis_size("dp")
    share = channels // pieces
    sub = round_up(rows + 2, SUB)
    padded = round_up(channels, LANES)
    slot = padded // pieces
    me = lax.axis_index("slab")
    where = me.astype(jnp.int32).reshape(1)
    even = me % 2 == 0
    image = inputs.reshape(rows, flat)
    cotangent = upstream.reshape(rows, flat)
    near = [(i, i ^ 1) for i in range(pieces)]
    far = [(i, (i - 1) % pieces if i % 2 == 0 else (i + 1) % pieces) for i in range(pieces)]
    one = lax.ppermute(lax.dynamic_slice_in_dim(image, jnp.where(even, rows - 1, 0), 1, 0), "slab", near)
    two = lax.ppermute(lax.dynamic_slice_in_dim(image, jnp.where(even, 0, rows - 1), 1, 0), "slab", far)

    def prepare(cw, *refs):
        prepare_kernel(pieces, [cw[t] for t in range(3)], *refs)

    lane3 = (cols, sub, channels)
    pixels = cols * sub
    raw, part, grad_out, grad_group, spread_weight = call(
        prepare,
        [(lane3, F32), (lane3, F32), (lane3, F32), ((pixels, padded), F32), ((channels, padded), BF16)],
        class_weights, image, cotangent, labels.reshape(rows, cols), depth_kernel, point_weight,
        smem=(0,),
    )
    depth, projected, active, stats = call(
        lambda *refs: forward_kernel(pieces, *refs, rows),
        [((pixels, channels), BF16), ((pixels, padded), F32), (lane3, F32), ((SUB, padded), F32)],
        where, part, raw, one, two, depth_kernel, spread_weight, grad_group,
        smem=(0,),
        scratch=[pltpu.VMEM(lane3, F32)],
    )
    other_depth = lax.ppermute(depth, "slab", near)
    all_stats = lax.all_gather(stats, "slab", axis=0, tiled=True)
    full, keep, send, norm = call(
        functools.partial(cotangent_kernel, pieces, rows, cols),
        [((pixels, padded), BF16), ((pixels, padded // 2), BF16), ((pixels, padded // 2), BF16), ((SUB, padded), F32)],
        where, all_stats, projected, grad_group, gain.reshape(1, -1), shift.reshape(1, -1),
        smem=(0,),
    )
    theirs = lax.ppermute(send, "slab", near)
    depth_grad, taps, edge_one, edge_two = call(
        functools.partial(backward_kernel, rows),
        [(lane3, F32), ((2 * SUB, channels), F32), ((cols, channels), BF16), ((cols, channels), BF16)],
        full, spread_weight, active, where,
        smem=(3,),
    )
    (blocks,) = call(product_kernel, [((padded // 2, channels), F32)], keep, theirs, depth, other_depth)
    blocks = blocks.reshape(pieces // 2, slot, channels)
    while blocks.shape[0] > 1:
        half = blocks.shape[0] // 2
        high = ((me // 2) & half) != 0
        mine = lax.dynamic_slice_in_dim(blocks, jnp.where(high, half, 0), half, 0)
        other = lax.dynamic_slice_in_dim(blocks, jnp.where(high, 0, half), half, 0).astype(BF16)
        came = lax.ppermute(other, "slab", [(i, i ^ (2 * half)) for i in range(pieces)])
        blocks = mine + came.astype(F32)
    block = blocks[0]
    tap_sum = jnp.sum(lax.all_gather(taps, "slab", axis=0), axis=0)[:9]
    tap_share = lax.dynamic_slice_in_dim(tap_sum, me * share, share, 1)
    place = jnp.where(even, me // 2, pieces // 2 + me // 2) * slot
    group = lax.dynamic_slice_in_dim(norm[4:6], place, share, 1)
    small = jnp.concatenate([tap_share, group], axis=0)
    high, low = high_low(small)
    count = 2 * small.shape[0]
    packed = jnp.concatenate([high, low], axis=0).reshape(-1)
    extra = round_up(count * share, channels) // channels
    packed = jnp.pad(packed, (0, extra * channels - count * share)).reshape(extra, channels)
    total = round_up(share + extra, copies)
    piece = total // copies
    payload = jnp.concatenate([block[:share].astype(BF16), packed], axis=0)
    payload = jnp.pad(payload, ((0, total - payload.shape[0]), (0, 0))).reshape(copies, piece, channels)
    landed = lax.all_to_all(payload, "dp", 0, 0)
    summed = jnp.sum(landed.astype(F32), axis=0)
    gathered = lax.all_to_all(jnp.broadcast_to(summed.astype(BF16)[None], payload.shape), "dp", 0, 0)
    batch = samples * copies
    result = gathered.reshape(total, channels).astype(F32) / batch
    point_out = result[:share].T
    rest = result[share : share + extra].reshape(-1)[: count * share].reshape(2, small.shape[0], share)
    rest = rest[0] + rest[1]

    halo_one = lax.ppermute(edge_one, "slab", near)
    halo_two = lax.ppermute(edge_two, "slab", far)
    block_out, grad_input = call(
        functools.partial(output_kernel, pieces, rows),
        [((rows, flat), BF16), ((rows, flat), BF16)],
        where, raw, grad_out, projected, norm, depth_grad, halo_one, halo_two, depth_kernel,
        smem=(0,),
        scratch=[pltpu.VMEM(lane3, F32), pltpu.VMEM((sub, flat), F32), pltpu.VMEM((sub, flat), F32)],
    )
    return (
        block_out.reshape(inputs.shape),
        grad_input.reshape(inputs.shape),
        point_out,
        rest[:9],
        rest[9],
        rest[10],
    )


def solution(mesh):
    return jax.shard_map(
        local,
        mesh=mesh,
        in_specs=(
            P("dp", "slab", None),
            P("dp", "slab", None),
            P("dp", "slab", None),
            P(),
            P(),
            P(),
            P(),
            P(),
        ),
        out_specs=(
            P("dp", "slab", None),
            P("dp", "slab", None),
            P(None, "slab"),
            P(None, "slab"),
            P("slab"),
            P("slab"),
        ),
        check_vma=False,
    )
```

time: 209 us -> 100 us (0.48)
  waiting for transfers between devices: 69.5 us -> 9.96 us
  blocking collectives: 71.1 us -> 27.1 us
  Pallas kernels: 0 us -> 17.5 us
  between operations: 15.3 us -> 0.87 us
  other arithmetic: 16.7 us -> 3.73 us
  local copies, waits for them, and re-layouts: 19.8 us -> 31.2 us
  matrix products: 6.02 us -> 0 us
    psum x1 -> x0, waiting for transfers between devices: 66.4 us -> none  [local(): lax.psum((point_share, tap_share, gain_share, shift_share), 'dp')]
    psum x3 -> x0, blocking collectives: 58.5 us -> none  [the longest x1 37.4 us: local(): lax.psum((point_share, tap_share, gain_share, shift_share), 'dp')]
    pallas_call x0 -> x6, Pallas kernels: none -> 17.5 us  [call(): pl.pallas_call(body, out_shape=[jax.ShapeDtypeStruct(shape, dtype) for sh...]
    all_to_all x0 -> x1, blocking collectives: none -> 15.9 us  [local(): landed = lax.all_to_all(payload, 'dp', 0, 0)]
    unnamed x64 -> x61, local copies, waits for them, and re-layouts: 2.74 us -> 18.1 us
    unnamed x1 -> x0, blocking collectives: 12.6 us -> none
    all_gather x0 -> x2, blocking collectives: none -> 11.1 us  [the longest x1 5.59 us: local(): tap_sum = jnp.sum(lax.all_gather(taps, 'slab', axis=0), axis=0)[:9]]
    ppermute x4 -> x7, waiting for transfers between devices: 0.01 us -> 9.96 us  [the longest x1 6.31 us: local(): lax.ppermute(other, 'slab', [(i, i ^ 2 * half) for i in range(pieces)])]
  transfers between devices with their start and end apart: 7 -> 8, of which waited for: 2 -> 3; matrix products, arithmetic and copies ran while one was open for 14% -> 6% of each run, Pallas kernels for 0% -> 13%
where the time goes in v1:
time: 100 us; the launch traced here: 99.2 us
  local copies, waits for them, and re-layouts  31.2 us (31%)
  blocking collectives  27.1 us (27%)
  Pallas kernels  17.5 us (18%)
  waiting for transfers between devices  9.96 us (10%)
  starting transfers between devices  8.92 us (9%)
  other arithmetic  3.73 us (4%)
    unnamed x61, local copies, waits for them, and re-layouts  18.1 us
    pallas_call x6, Pallas kernels, call(): pl.pallas_call(body, out_shape=[jax.ShapeDtypeStruct(shape, dtype) for sh...  17.5 us
    all_to_all x1, blocking collectives, local(): landed = lax.all_to_all(payload, 'dp', 0, 0)  15.9 us
    ppermute x1, waiting for transfers between devices, local(): lax.ppermute(other, 'slab', [(i, i ^ 2 * half) for i in range(pieces)])  6.31 us
    all_gather x1, blocking collectives, local(): tap_sum = jnp.sum(lax.all_gather(taps, 'slab', axis=0), axis=0)[:9]  5.59 us
    all_gather x1, blocking collectives, local(): all_stats = lax.all_gather(stats, 'slab', axis=0, tiled=True)  5.55 us
    all_to_all x1, starting transfers between devices, local(): lax.all_to_all(jnp.broadcast_to(summed.astype(BF16)[None], payload.shape)...  4.24 us
    ppermute x1, waiting for transfers between devices, local(): halo_two = lax.ppermute(edge_two, 'slab', far)  2.8 us
  transfers between devices with their start and end apart: 8, of which 3 were waited for; matrix products, arithmetic and copies ran while one was open for 6% of the time, Pallas kernels for 13%

profile of v1, /device:TPU:0, one launch (start us, length us, event | category | flops | bytes accessed | tf_op | source)
XLA Modules:
  0.0 99.2 jit_solution(17119631583578713930)
XLA Ops:
  0.7 1.5 %dynamic-slice_bitcast_fusion = (bf16[1,34944]{1,0:T(2,128)(2,1)S(1)}, bf16[1,34944]{1,0:T(2,128)(2,1)S(1)}) fusion(bf16[1,6,34944]{2,1,0:T(8,128)(2,1)} %param.8, s32[]{:T(128)S(6)} %select_n.41, s32[]{:T(128)S(6)} %select_n.40), kind=kLoop, calls=%fused_computation.10 | loop fusion | bytes 279560 | tf_op jit(solution)/shard_map/dynamic_slice | solution.py:301
  2.7 2.6 %collective-permute-start.1 = (bf16[1,34944]{1,0:T(2,128)(2,1)S(1)}, bf16[1,34944]{1,0:T(2,128)(2,1)S(1)}, u32[]{:S(2)}, u32[]{:S(2)}) collective-permute-start(bf16[1,34944]{1,0:T(2,128)(2,1)S(1)} %get-tuple-element.44), channel_id=1, source_target_pairs={{0,3},{1,2},{2,1},{3,0},{4,7},{5,6},{6,5},{7,4},{8,11},{9,10},{10,... | collective-permute-start | bytes 209672 | tf_op jit(solution)/shard_map/ppermute | solution.py:301
  6.0 1.1 %copy-done.5 = bf16[1,6,34944]{2,1,0:T(8,128)(2,1)S(1)} copy-done((bf16[1,6,34944]{2,1,0:T(8,128)(2,1)S(1)}, bf16[1,6,34944]{2,1,0:T(8,128)(2,1)}, u32[]{:S(2)}) %copy-start.5) | copy-done | bytes 419352
  7.1 1.2 %copy-done.12 = bf16[728,728]{1,0:T(8,128)(2,1)S(1)} copy-done((bf16[728,728]{1,0:T(8,128)(2,1)S(1)}, bf16[728,728]{1,0:T(8,128)(2,1)}, u32[]{:S(2)}) %copy-start.12) | copy-done | bytes 1059992
  8.3 1.1 %copy-done.13 = bf16[1,6,34944]{2,1,0:T(8,128)(2,1)S(1)} copy-done((bf16[1,6,34944]{2,1,0:T(8,128)(2,1)S(1)}, bf16[1,6,34944]{2,1,0:T(8,128)(2,1)}, u32[]{:S(2)}) %copy-start.13) | copy-done | bytes 419352
  10.8 4.9 %shard_map.127 = (f32[48,8,728]{2,1,0:T(8,128)S(1)}, f32[48,8,728]{2,1,0:T(8,128)S(1)}, f32[48,8,728]{2,1,0:T(8,128)S(1)}, f32[384,768]{1,0:T(8,128)S(1)}, bf16[728,768]{1,0:T(8,128)(2,1)S(1)}) custom-call(f32[3]{0:T(128)S(1)} %copy-done.23, bf16[6,34944]{1,0:T(8,128)(2,1)S(1)} %bitcast.26, bf16[6,34944]{1,0:T(8,128)(2,1)S(1)} %bitcast.27, ...), custom_call_target="tpu_custom_call" | custom-call | tf_op jit(solution)/shard_map/pallas_call | solution.py:272
  15.7 1.0 %copy-done.6 = f32[48,8,728]{2,1,0:T(8,128)} copy-done((f32[48,8,728]{2,1,0:T(8,128)}, f32[48,8,728]{2,1,0:T(8,128)S(1)}, u32[]{:S(2)}) %copy-start.6) | copy-done | bytes 1118232
  16.8 3.9 %shard_map.128 = (bf16[384,728]{1,0:T(8,128)(2,1)S(1)}, f32[384,768]{1,0:T(8,128)S(1)}, f32[48,8,728]{2,1,0:T(8,128)S(1)}, f32[8,768]{1,0:T(8,128)S(1)}) custom-call(s32[1]{0:T(128)} %bitcast.refs_0_.where_ref, f32[48,8,728]{2,1,0:T(8,128)S(1)} %get-tuple-element.27.refs_1_, f32[48,8,728]{2,1,0:T(8,128)S(1)} %get-tuple-element.25.refs_2_.image_ref, ...), custom_call_target="tpu_custom_call" | custom-call | tf_op jit(solution)/shard_map/pallas_call | solution.py:272
  21.6 1.0 %copy-done.10 = f32[48,8,728]{2,1,0:T(8,128)} copy-done((f32[48,8,728]{2,1,0:T(8,128)}, f32[48,8,728]{2,1,0:T(8,128)S(1)}, u32[]{:S(2)}) %copy-start.10) | copy-done | bytes 1118232
  23.2 2.1 %copy.14 = bf16[384,728]{0,1:T(8,128)(2,1)} copy(bf16[384,728]{1,0:T(8,128)(2,1)} %copy-done.2) | data formatting | bytes 1118208 | tf_op jit(solution)/shard_map/pallas_call | solution.py:272
  25.4 5.5 %all_gather.9.stats_ref = f32[32,768]{1,0:T(8,128)S(1)} all-gather(f32[8,768]{1,0:T(8,128)} %copy-done.22), channel_id=1, replica_groups=mesh['dp'=8,'slab'=4] {'slab'}, dimensions={0}, use_global_device_ids=true | all-gather | bytes 122880 | tf_op jit(solution)/shard_map/all_gather | solution.py:322
  31.0 1.3 %shard_map.129 = (bf16[384,768]{1,0:T(8,128)(2,1)S(1)}, bf16[384,384]{1,0:T(8,128)(2,1)S(1)}, bf16[384,384]{1,0:T(8,128)(2,1)}, f32[8,768]{1,0:T(8,128)S(1)}) custom-call(s32[1]{0:T(128)} %bitcast.refs_0_.where_ref, f32[32,768]{1,0:T(8,128)S(1)} %all_gather.9.stats_ref, f32[384,768]{1,0:T(8,128)S(1)} %get-tuple-element.30.proj_ref, ...), custom_call_target="tpu_custom_call" | custom-call | tf_op jit(solution)/shard_map/pallas_call | solution.py:272
  33.3 1.8 %shard_map.130 = (f32[48,8,728]{2,1,0:T(8,128)S(1)}, f32[16,728]{1,0:T(8,128)S(1)}, bf16[48,728]{1,0:T(8,128)(2,1)S(1)}, bf16[48,728]{1,0:T(8,128)(2,1)S(1)}) custom-call(bf16[384,768]{1,0:T(8,128)(2,1)S(1)} %get-tuple-element.33.full_ref, bf16[728,768]{1,0:T(8,128)(2,1)S(1)} %copy-done.1, f32[48,8,728]{2,1,0:T(8,128)S(1)} %copy-done.11, ...), custom_call_target="tpu_custom_call" | custom-call | tf_op jit(solution)/shard_map/pallas_call | solution.py:272
  35.1 1.0 %copy-done.8 = f32[48,8,728]{2,1,0:T(8,128)} copy-done((f32[48,8,728]{2,1,0:T(8,128)}, f32[48,8,728]{2,1,0:T(8,128)S(1)}, u32[]{:S(2)}) %copy-start.8) | copy-done | bytes 1118232
  36.1 5.6 %all-gather = f32[64,728]{1,0:T(8,128)S(1)} all-gather(f32[16,728]{1,0:T(8,128)S(1)} %get-tuple-element.43), channel_id=2, replica_groups=mesh['dp'=8,'slab'=4] {'slab'}, dimensions={0}, use_global_device_ids=true | all-gather | bytes 232960 | tf_op jit(solution)/shard_map/all_gather | solution.py:346
  42.5 2.1 %copy.15.other_ref = bf16[384,728]{1,0:T(8,128)(2,1)} copy(bf16[384,728]{0,1:T(8,128)(2,1)} %collective-permute-done.5) | data formatting | bytes 1118208 | tf_op jit(solution)/shard_map/ppermute | solution.py:321
  45.3 1.1 %copy-done.3 = bf16[384,728]{1,0:T(8,128)(2,1)S(1)} copy-done((bf16[384,728]{1,0:T(8,128)(2,1)S(1)}, bf16[384,728]{1,0:T(8,128)(2,1)}, u32[]{:S(2)}) %copy-start.3) | copy-done | bytes 559128
  46.4 1.1 %copy-done.4 = bf16[384,728]{1,0:T(8,128)(2,1)S(1)} copy-done((bf16[384,728]{1,0:T(8,128)(2,1)S(1)}, bf16[384,728]{1,0:T(8,128)(2,1)}, u32[]{:S(2)}) %copy-start.4) | copy-done | bytes 559128
  47.4 1.0 copy-done.15
  48.4 1.0 copy-done.17
  52.1 1.3 %pad.8 = bf16[4368]{0:T(1024)(128)(2,1)} pad(bf16[4004]{0:T(1024)(128)(2,1)} %reshape.78, bf16[]{:T(256)} %constant.57.clone.1), padding=0_364 | pad | bytes 16746 | tf_op jit(solution)/shard_map/jit(_pad)/pad | solution.py:355
  54.2 6.3 %collective-permute-done.6 = bf16[1,192,728]{2,1,0:T(8,128)(2,1)} collective-permute-done((bf16[1,192,728]{2,1,0:T(8,128)(2,1)}, bf16[1,192,728]{2,1,0:T(8,128)(2,1)}, u32[]{:S(2)}, u32[]{:S(2)}) %collective-permute-start.6) | collective-permute-done | bytes 279584 | tf_op jit(solution)/shard_map/ppermute | solution.py:343
  60.5 1.0 %fusion.4 = bf16[182,728]{1,0:T(8,128)(2,1)S(1)} fusion(f32[2,192,728]{2,1,0:T(8,128)S(1)} %bitcast.25, s32[]{:T(128)S(6)} %select_n.43, bf16[1,192,728]{2,1,0:T(8,128)(2,1)} %collective-permute-done.6), kind=kLoop, calls=%fused_computation.9 | loop fusion | flops 397488 | bytes 1059972 | tf_op jit(solution)/shard_map/convert_element_type | solution.py:358
  61.5 15.9 %all_to_all.10 = bf16[8,24,728]{2,1,0:T(8,128)(2,1)} all-to-all(bf16[8,24,728]{2,1,0:T(8,128)(2,1)S(1)} %bitcast.31), channel_id=1, replica_groups=mesh['dp'=8,'slab'=4] {'dp'}, dimensions={0} | all-to-all | bytes 559104 | tf_op jit(solution)/shard_map/all_to_all | solution.py:360
  77.5 1.6 %reduce_sum.22 = bf16[24,728]{1,0:T(8,128)(2,1)} reduce(bf16[8,24,728]{2,1,0:T(8,128)(2,1)} %all_to_all.10, bf16[]{:T(256)} %constant.57.clone.1), dimensions={0}, to_apply=%region_1.2 | reduce | flops 122304 | bytes 314498 | tf_op jit(solution)/shard_map/reduce_sum | solution.py:361
  79.1 1.5 %broadcast_in_dim.2 = bf16[8,24,728]{2,1,0:T(8,128)(2,1)} broadcast(bf16[24,728]{1,0:T(8,128)(2,1)} %reduce_sum.22), dimensions={1,2} | broadcast | bytes 314496 | tf_op jit(solution)/shard_map/broadcast_in_dim | solution.py:362
  80.6 4.2 %all-to-all-start.1 = ((bf16[8,24,728]{2,1,0:T(8,128)(2,1)}), bf16[8,24,728]{2,1,0:T(8,128)(2,1)}, u32[]{:S(2)}, u32[]{:S(2)}) async-start(bf16[8,24,728]{2,1,0:T(8,128)(2,1)} %broadcast_in_dim.2), calls=%async_computation.1 | async-start | bytes 589824 | tf_op jit(solution)/shard_map/all_to_all | solution.py:362
  86.4 2.8 %collective-permute-done.3.two_ref = bf16[48,728]{1,0:T(8,128)(2,1)S(1)} collective-permute-done((bf16[48,728]{1,0:T(8,128)(2,1)}, bf16[48,728]{1,0:T(8,128)(2,1)S(1)}, u32[]{:S(2)}, u32[]{:S(2)}) %collective-permute-start.3) | collective-permute-done | bytes 69920 | tf_op jit(solution)/shard_map/ppermute | solution.py:370
  89.2 1.3 %copy-done.9 = f32[48,8,728]{2,1,0:T(8,128)S(1)} copy-done((f32[48,8,728]{2,1,0:T(8,128)S(1)}, f32[48,8,728]{2,1,0:T(8,128)}, u32[]{:S(2)}) %copy-start.9) | copy-done | bytes 1118232
  91.9 4.7 %shard_map.131 = (bf16[6,34944]{1,0:T(8,128)(2,1)}, bf16[6,34944]{1,0:T(8,128)(2,1)}) custom-call(s32[1]{0:T(128)} %bitcast.refs_0_.where_ref, f32[48,8,728]{2,1,0:T(8,128)S(1)} %get-tuple-element.25.refs_2_.image_ref, f32[48,8,728]{2,1,0:T(8,128)S(1)} %copy-done.7, f32[384,768]{1,0:T(8,128)S(1)} %get-tuple-element.30.proj_ref, f32[8,768]{1,0:T(8,128)S(1)} %copy-done.21, ...), custom_call_target="tpu_custom_call" | custom-call | tf_op jit(solution)/shard_map/pallas_call | solution.py:272
  96.6 1.0 %convert_multiply_fusion = f32[8,24,728]{2,1,0:T(8,128)S(1)} fusion(bf16[8,24,728]{2,1,0:T(8,128)(2,1)} %all-to-all-done.1), kind=kLoop, calls=%fused_computation.3 | loop fusion | flops 279552 | bytes 838656 | tf_op jit(solution)/shard_map/div | solution.py:364
  97.6 0.8 slice_bitcast_fusion
  (80 shorter events, 13.8 us)
Async XLA Ops:
  2.2 14.6 %collective-permute-start = (bf16[1,34944]{1,0:T(2,128)(2,1)S(1)}, bf16[1,34944]{1,0:T(2,128)(2,1)S(1)}, u32[]{:S(2)}, u32[]{:S(2)}) collective-permute-start(bf16[1,34944]{1,0:T(2,128)(2,1)S(1)} %get-tuple-element.45), channel_id=1, source_target_pairs={{0,1},{1,0},{2,3},{3,2},{4,5},{5,4},{6,7},{7,6},{8,9},{9,8},{10,11... | collective-permute-start | bytes 209672 | tf_op jit(solution)/shard_map/ppermute | solution.py:300
  2.7 14.1 %collective-permute-start.1 = (bf16[1,34944]{1,0:T(2,128)(2,1)S(1)}, bf16[1,34944]{1,0:T(2,128)(2,1)S(1)}, u32[]{:S(2)}, u32[]{:S(2)}) collective-permute-start(bf16[1,34944]{1,0:T(2,128)(2,1)S(1)} %get-tuple-element.44), channel_id=1, source_target_pairs={{0,3},{1,2},{2,1},{3,0},{4,7},{5,6},{6,5},{7,4},{8,11},{9,10},{10,... | collective-permute-start | bytes 209672 | tf_op jit(solution)/shard_map/ppermute | solution.py:301
  6.0 1.1 %copy-start.5 = (bf16[1,6,34944]{2,1,0:T(8,128)(2,1)S(1)}, bf16[1,6,34944]{2,1,0:T(8,128)(2,1)}, u32[]{:S(2)}) copy-start(bf16[1,6,34944]{2,1,0:T(8,128)(2,1)} %param.8) | copy-start | bytes 1257988
  7.1 1.2 %copy-start.12 = (bf16[728,728]{1,0:T(8,128)(2,1)S(1)}, bf16[728,728]{1,0:T(8,128)(2,1)}, u32[]{:S(2)}) copy-start(bf16[728,728]{1,0:T(8,128)(2,1)} %refs_4_.1) | copy-start | bytes 3179908
  8.3 1.1 %copy-start.13 = (bf16[1,6,34944]{2,1,0:T(8,128)(2,1)S(1)}, bf16[1,6,34944]{2,1,0:T(8,128)(2,1)}, u32[]{:S(2)}) copy-start(bf16[1,6,34944]{2,1,0:T(8,128)(2,1)} %param.9) | copy-start | bytes 1257988
  9.4 0.7 copy-start.18
  15.7 1.0 %copy-start.6 = (f32[48,8,728]{2,1,0:T(8,128)}, f32[48,8,728]{2,1,0:T(8,128)S(1)}, u32[]{:S(2)}) copy-start(f32[48,8,728]{2,1,0:T(8,128)S(1)} %get-tuple-element.26.grad_ref) | copy-start | bytes 3354628
  16.7 4.0 %copy-start = (bf16[728,768]{1,0:T(8,128)(2,1)}, bf16[728,768]{1,0:T(8,128)(2,1)S(1)}, u32[]{:S(2)}) copy-start(bf16[728,768]{1,0:T(8,128)(2,1)S(1)} %get-tuple-element.28.refs_6_.spread_ref) | copy-start | bytes 3354628
  16.8 8.6 %copy-start.28 = (f32[728]{0:T(1024)S(1)}, f32[728]{0:T(1024)}, u32[]{:S(2)}) copy-start(f32[728]{0:T(1024)} %param.14) | copy-start | bytes 8740
  20.7 0.8 copy-start.2
  21.5 1.0 %copy-start.10 = (f32[48,8,728]{2,1,0:T(8,128)}, f32[48,8,728]{2,1,0:T(8,128)S(1)}, u32[]{:S(2)}) copy-start(f32[48,8,728]{2,1,0:T(8,128)S(1)} %get-tuple-element.34.active_ref) | copy-start | bytes 3354628
  23.2 2.2 %copy-start.29 = (f32[728]{0:T(1024)S(1)}, f32[728]{0:T(1024)}, u32[]{:S(2)}) copy-start(f32[728]{0:T(1024)} %param.15) | copy-start | bytes 8740
  25.3 17.2 %collective-permute-start.5 = (bf16[384,728]{0,1:T(8,128)(2,1)}, bf16[384,728]{0,1:T(8,128)(2,1)}, u32[]{:S(2)}, u32[]{:S(2)}) collective-permute-start(bf16[384,728]{0,1:T(8,128)(2,1)} %copy.14), channel_id=1, source_target_pairs={{0,1},{1,0},{2,3},{3,2},{4,5},{5,4},{6,7},{7,6},{8,9},{9,8},{10,11... | collective-permute-start | bytes 1677320 | tf_op jit(solution)/shard_map/ppermute | solution.py:321
  30.9 2.3 %copy-start.1 = (bf16[728,768]{1,0:T(8,128)(2,1)S(1)}, bf16[728,768]{1,0:T(8,128)(2,1)}, u32[]{:S(2)}) copy-start(bf16[728,768]{1,0:T(8,128)(2,1)} %copy-done) | copy-start | bytes 3354628
  31.0 2.3 %copy-start.11 = (f32[48,8,728]{2,1,0:T(8,128)S(1)}, f32[48,8,728]{2,1,0:T(8,128)}, u32[]{:S(2)}) copy-start(f32[48,8,728]{2,1,0:T(8,128)} %copy-done.10) | copy-start | bytes 3354628
  32.3 2.8 %copy-start.14 = (bf16[384,384]{1,0:T(8,128)(2,1)}, bf16[384,384]{1,0:T(8,128)(2,1)S(1)}, u32[]{:S(2)}) copy-start(bf16[384,384]{1,0:T(8,128)(2,1)S(1)} %get-tuple-element.40.mine_ref) | copy-start | bytes 884740
  32.9 11.7 %collective-permute-start.4 = (bf16[384,384]{1,0:T(8,128)(2,1)}, bf16[384,384]{1,0:T(8,128)(2,1)S(1)}, u32[]{:S(2)}, u32[]{:S(2)}) collective-permute-start(bf16[384,384]{1,0:T(8,128)(2,1)} %get-tuple-element.41), channel_id=1, source_target_pairs={{0,1},{1,0},{2,3},{3,2},{4,5},{5,4},{6,7},{7,6},{8,9},{9,8},{10,11... | collective-permute-start | bytes 884744 | tf_op jit(solution)/shard_map/ppermute | solution.py:329
  35.1 1.0 %copy-start.8 = (f32[48,8,728]{2,1,0:T(8,128)}, f32[48,8,728]{2,1,0:T(8,128)S(1)}, u32[]{:S(2)}) copy-start(f32[48,8,728]{2,1,0:T(8,128)S(1)} %get-tuple-element.35.depth_grad_ref) | copy-start | bytes 3354628
  36.1 5.6 %copy-start.24 = (bf16[48,728]{1,0:T(8,128)(2,1)}, bf16[48,728]{1,0:T(8,128)(2,1)S(1)}, u32[]{:S(2)}) copy-start(bf16[48,728]{1,0:T(8,128)(2,1)S(1)} %get-tuple-element.37) | copy-start | bytes 209668
  36.1 5.6 %copy-start.25 = (bf16[48,728]{1,0:T(8,128)(2,1)}, bf16[48,728]{1,0:T(8,128)(2,1)S(1)}, u32[]{:S(2)}) copy-start(bf16[48,728]{1,0:T(8,128)(2,1)S(1)} %get-tuple-element.36) | copy-start | bytes 209668
  45.3 1.1 %copy-start.3 = (bf16[384,728]{1,0:T(8,128)(2,1)S(1)}, bf16[384,728]{1,0:T(8,128)(2,1)}, u32[]{:S(2)}) copy-start(bf16[384,728]{1,0:T(8,128)(2,1)} %copy-done.2) | copy-start | bytes 1677316
  46.4 1.1 %copy-start.4 = (bf16[384,728]{1,0:T(8,128)(2,1)S(1)}, bf16[384,728]{1,0:T(8,128)(2,1)}, u32[]{:S(2)}) copy-start(bf16[384,728]{1,0:T(8,128)(2,1)} %copy.15.other_ref) | copy-start | bytes 1677316
  47.4 1.0 copy-start.15
  48.4 1.0 copy-start.17
  49.3 2.0 %copy-start.27 = (f32[2,182]{1,0:T(2,128)S(1)}, f32[2,182]{1,0:T(2,128)}, u32[]{:S(2)}) copy-start(f32[2,182]{1,0:T(2,128)} %constant_dynamic-slice_fusion) | copy-start | bytes 4372
  50.9 9.6 %collective-permute-start.6 = (bf16[1,192,728]{2,1,0:T(8,128)(2,1)}, bf16[1,192,728]{2,1,0:T(8,128)(2,1)}, u32[]{:S(2)}, u32[]{:S(2)}) collective-permute-start(bf16[1,192,728]{2,1,0:T(8,128)(2,1)} %dynamic-slice_convert_fusion), channel_id=1, source_target_pairs={{0,2},{1,3},{2,0},{3,1},{4,6},{5,7},{6,4},{7,5},{8,10},{9,11},{10,... | collective-permute-start | bytes 838664 | tf_op jit(solution)/shard_map/ppermute | solution.py:343
  61.5 27.7 %copy-start.7 = (f32[48,8,728]{2,1,0:T(8,128)S(1)}, f32[48,8,728]{2,1,0:T(8,128)}, u32[]{:S(2)}) copy-start(f32[48,8,728]{2,1,0:T(8,128)} %copy-done.6) | copy-start | bytes 3354628
  80.6 16.1 %all-to-all-start.1 = ((bf16[8,24,728]{2,1,0:T(8,128)(2,1)}), bf16[8,24,728]{2,1,0:T(8,128)(2,1)}, u32[]{:S(2)}, u32[]{:S(2)}) async-start(bf16[8,24,728]{2,1,0:T(8,128)(2,1)} %broadcast_in_dim.2), calls=%async_computation.1 | async-start | bytes 589824 | tf_op jit(solution)/shard_map/all_to_all | solution.py:362
  84.8 1.5 %collective-permute-start.2 = (bf16[48,728]{1,0:T(8,128)(2,1)}, bf16[48,728]{1,0:T(8,128)(2,1)S(1)}, u32[]{:S(2)}, u32[]{:S(2)}) collective-permute-start(bf16[48,728]{1,0:T(8,128)(2,1)} %copy-done.25), channel_id=1, source_target_pairs={{0,1},{1,0},{2,3},{3,2},{4,5},{5,4},{6,7},{7,6},{8,9},{9,8},{10,11... | collective-permute-start | bytes 209672 | tf_op jit(solution)/shard_map/ppermute | solution.py:369
  84.9 4.3 %collective-permute-start.3 = (bf16[48,728]{1,0:T(8,128)(2,1)}, bf16[48,728]{1,0:T(8,128)(2,1)S(1)}, u32[]{:S(2)}, u32[]{:S(2)}) collective-permute-start(bf16[48,728]{1,0:T(8,128)(2,1)} %copy-done.24), channel_id=1, source_target_pairs={{0,3},{1,2},{2,1},{3,0},{4,7},{5,6},{6,5},{7,4},{8,11},{9,10},{10,... | collective-permute-start | bytes 209672 | tf_op jit(solution)/shard_map/ppermute | solution.py:370
  89.2 1.3 %copy-start.9 = (f32[48,8,728]{2,1,0:T(8,128)S(1)}, f32[48,8,728]{2,1,0:T(8,128)}, u32[]{:S(2)}) copy-start(f32[48,8,728]{2,1,0:T(8,128)} %copy-done.8) | copy-start | bytes 3354628
  91.2 0.7 copy-start.21
  (6 other events, 4.0 us)
